TPU v7x, 32 devices: a whole 2x2x4 slice. The times are simulated.
32 devices in a mesh: row: 8 (over z, core), col: 4 (over y, x).
Axes of the slice: x: 2, y: 2, z: 4, core: 2. Of those that a mesh axis runs over, the one named last changes fastest.
Arguments:
- density: float32 [96, 13, 128, 128], P('row', None, 'col'), may hold values from -1.5 to 1.5
- pattern: int32 [96, 13], P('row'), may hold values from 0 to 1, as said below
Outputs:
- purified: float32 [96, 13, 128, 128], P('row', None, 'col')
Inputs may be any that keep to these rules, and one draw needn't show every extreme that they name: `pattern`: each block row has exactly 7 ones, placed at random slots.
All inputs are finite; a program needn't handle non-finite values.
Results may differ from a plain program's by a relative error of at most 0.0003.
Values sent between devices are 32-bit elements; how exact they have to be, the bound alone decides.
A program may use at most 64 MiB of HBM per device.

v0:
```python
import jax
import jax.numpy as jnp
from jax import lax
from jax.sharding import PartitionSpec as P


def with_halo(cells, sides, width):
    for axis, dim in sides:
        count = lax.axis_size(axis)
        head = lax.slice_in_dim(cells, 0, width, axis=dim)
        tail = lax.slice_in_dim(cells, cells.shape[dim] - width, cells.shape[dim], axis=dim)
        cells = jnp.concatenate(
            [
                lax.ppermute(tail, axis, [(i, (i + 1) % count) for i in range(count)]),
                cells,
                lax.ppermute(head, axis, [((i + 1) % count, i) for i in range(count)]),
            ],
            axis=dim,
        )
    return cells


def shards(density, pattern):
    block_rows, band_slots, shard_cols, block_size = density.shape
    half_band = (band_slots - 1) // 2
    span_slots = 2 * band_slots - 1
    masked = density * pattern[:, :, None, None].astype(jnp.float32)
    slot_range = jnp.arange(band_slots, dtype=jnp.int32)
    slot_list = jnp.broadcast_to(slot_range[None, :], (block_rows, band_slots))
    extended = with_halo(masked, (("row", 0),), half_band)
    row_range = jnp.arange(block_rows, dtype=jnp.int32)
    span_range = jnp.arange(span_slots, dtype=jnp.int32)
    panel_piece = lax.all_gather(masked, "col", axis=2, tiled=True)

    def square_one_row(row_index):
        left_blocks = panel_piece[row_index]
        offsets = slot_list[row_index]
        right_blocks = extended[row_index + offsets]
        products = jnp.einsum(
            "sca,sdbc->sdba", left_blocks, right_blocks, precision=lax.Precision.HIGHEST
        )
        slot_place = (
            (offsets[:, None] + slot_range[None, :])[:, :, None] == span_range[None, None, :]
        ).astype(jnp.float32)
        return jnp.einsum("sdba,sde->eba", products, slot_place, precision=lax.Precision.HIGHEST)

    square = lax.map(square_one_row, row_range)
    square_ext = with_halo(square, (("row", 0),), half_band)
    cube_panel_piece = lax.all_gather(masked, "col", axis=2, tiled=True)

    def cube_one_row(row_index):
        left_blocks = cube_panel_piece[row_index]
        offsets = slot_list[row_index]
        columns = 2 * half_band - offsets[:, None] + slot_range[None, :]
        right_blocks = square_ext[(row_index + offsets)[:, None], columns]
        return jnp.einsum(
            "sca,sibc->iba", left_blocks, right_blocks, precision=lax.Precision.HIGHEST
        )

    third_power = lax.map(cube_one_row, row_range)
    band_core = square[:, half_band : half_band + band_slots]
    return (3.0 * band_core - 2.0 * third_power) * pattern[:, :, None, None].astype(jnp.float32)


def solution(mesh):
    placed = (P("row", None, "col", None), P("row", None))
    return jax.shard_map(
        shards, mesh=mesh, in_specs=placed, out_specs=P("row", None, "col", None), check_vma=False
    )
```

profile of v0, /device:TPU:0, one launch (start us, length us, event | category | flops | bytes accessed | tf_op | source)
XLA Modules:
  0.0 520.2 jit_solution(9023532762369583053)
XLA Ops:
  7.2 3.4 broadcast_multiply_fusion
  14.6 4.0 collective-permute-start.1
  18.6 26.3 %collective-permute-done = f32[6,13,32,128]{3,2,1,0:T(8,128)} collective-permute-done((f32[6,13,32,128]{3,2,1,0:T(8,128)}, f32[6,13,32,128]{3,2,1,0:T(8,128)}, u32[]{:S(2)}, u32[]{:S(2)}) %collective-permute-start) | collective-permute-done | bytes 1277984 | tf_op jit(solution)/shard_map/ppermute | solution.py:14
  45.4 4.7 pad_maximum_fusion.1
  50.1 66.3 %all-gather.2.cloned.1.call-done = f32[12,13,128,128]{3,2,1,0:T(8,128)} async-done(((f32[12,13,32,128]{3,2,1,0:T(8,128)}), f32[12,13,128,128]{3,2,1,0:T(8,128)}) %all-gather.2.cloned.1.call-update) | async-done | bytes 10223632 | tf_op jit(solution)/shard_map/all_gather | solution.py:33
  116.4 171.0 %while.22 = (s32[]{:T(128)}, f32[12,25,32,128]{3,2,1,0:T(8,128)}, s32[12]{0:T(128)S(1)}, s32[12,13]{1,0:T(8,128)S(1)}, f32[24,13,32,128]{3,2,1,0:T(8,128)}, /*in...) while((s32[]{:T(128)}, f32[12,25,32,128]{3,2,1,0:T(8,128)}, s32[12]{0:T(128)S(1)}, ...), condition=%wide.region_1.2_spmd.clone, body=%wide.region_0.1_spmd.clone.sunk | while | flops 1270928768 | bytes 15931727 | solution.py:47
  122.8 3.8 fusion.51
  137.1 3.9 fusion.51
  151.3 3.8 fusion.51
  165.6 3.8 fusion.51
  179.9 3.8 fusion.51
  194.1 3.8 fusion.51
  208.4 3.9 fusion.51
  222.6 3.9 fusion.51
  236.9 3.9 fusion.51
  251.1 3.8 fusion.51
  265.4 3.8 fusion.51
  279.6 3.9 fusion.51
  287.5 5.2 %fusion.29 = (f32[6,25,32,128]{3,2,1,0:T(8,128)}, f32[6,25,32,128]{3,2,1,0:T(8,128)}) fusion(f32[12,25,32,128]{3,2,1,0:T(8,128)} %get-tuple-element.84), kind=kLoop, calls=%fused_computation.41 | loop fusion | bytes 9830400 | tf_op jit(solution)/shard_map/slice | solution.py:11
  292.7 3.5 collective-permute-start.3
  296.3 52.2 %collective-permute-done.2 = f32[6,25,32,128]{3,2,1,0:T(8,128)S(1)} collective-permute-done((f32[6,25,32,128]{3,2,1,0:T(8,128)}, f32[6,25,32,128]{3,2,1,0:T(8,128)S(1)}, u32[]{:S(2)}, u32[]{:S(2)}) %collective-permute-start.2) | collective-permute-done | bytes 2457632 | tf_op jit(solution)/shard_map/ppermute | solution.py:14
  348.5 8.2 %pad_maximum_fusion = f32[24,25,32,128]{3,2,1,0:T(8,128)} fusion(f32[6,25,32,128]{3,2,1,0:T(8,128)} %collective-permute-done.3, f32[12,25,32,128]{3,2,1,0:T(8,128)} %get-tuple-element.84, f32[6,25,32,128]{3,2,1,0:T(8,128)S(1)} %collective-permute-done.2), kind=kLoop, calls=%fused_computation.37 | loop fusion | flops 4915200 | bytes 19660800 | tf_op jit(solution)/shard_map/concatenate | solution.py:12
  356.7 152.3 %while.23 = (s32[]{:T(128)}, f32[12,13,32,128]{3,2,1,0:T(8,128)}, s32[12]{0:T(128)S(1)}, s32[12,13]{1,0:T(8,128)S(1)}, f32[24,25,32,128]{3,2,1,0:T(8,128)}, /*in...) while((s32[]{:T(128)}, f32[12,13,32,128]{3,2,1,0:T(8,128)}, s32[12]{0:T(128)S(1)}, ...), condition=%wide.region_3.4_spmd.clone, body=%wide.region_2.3_spmd.clone.sunk | while | flops 1063257344 | bytes 9376007 | solution.py:60
  360.0 5.2 gather_fusion.1
  365.1 4.2 fusion.58
  372.7 5.2 gather_fusion.1
  377.8 4.2 fusion.58
  385.4 5.2 gather_fusion.1
  390.5 4.2 fusion.58
  398.1 5.2 gather_fusion.1
  403.2 4.2 fusion.58
  410.7 5.2 gather_fusion.1
  415.9 4.2 fusion.58
  423.4 5.2 gather_fusion.1
  428.6 4.2 fusion.58
  436.1 5.2 gather_fusion.1
  441.3 4.2 fusion.58
  448.8 5.2 gather_fusion.1
  454.0 4.2 fusion.58
  461.5 5.2 gather_fusion.1
  466.7 4.2 fusion.58
  474.2 5.2 gather_fusion.1
  479.4 4.2 fusion.58
  486.9 5.2 gather_fusion.1
  492.1 4.2 fusion.58
  499.6 5.2 gather_fusion.1
  504.8 4.2 fusion.58
  509.0 4.3 subtract_multiply_fusion
  (172 shorter events, 122.9 us)
Async XLA Ops:
  6.5 109.9 %all-gather.2.cloned.1.call-start = ((), (), s32[]{:S(2)}) async-start(), calls=%async_computation | async-start | bytes 12779520 | tf_op jit(solution)/shard_map/all_gather | solution.py:33
  10.7 1.7 copy-start
  14.1 30.8 %collective-permute-start = (f32[6,13,32,128]{3,2,1,0:T(8,128)}, f32[6,13,32,128]{3,2,1,0:T(8,128)}, u32[]{:S(2)}, u32[]{:S(2)}) collective-permute-start(f32[6,13,32,128]{3,2,1,0:T(8,128)} %get-tuple-element.141), channel_id=1, source_target_pairs={{0,4},{4,8},{8,12},{12,16},{16,20},{20,24},{24,28},{28,0},{1,5},{5... | collective-permute-start | bytes 3833864 | tf_op jit(solution)/shard_map/ppermute | solution.py:14
  14.6 30.8 %collective-permute-start.1 = (f32[6,13,32,128]{3,2,1,0:T(8,128)}, f32[6,13,32,128]{3,2,1,0:T(8,128)}, u32[]{:S(2)}, u32[]{:S(2)}) collective-permute-start(f32[6,13,32,128]{3,2,1,0:T(8,128)} %get-tuple-element.142), channel_id=1, source_target_pairs={{4,0},{8,4},{12,8},{16,12},{20,16},{24,20},{28,24},{0,28},{5,1},{9... | collective-permute-start | bytes 3833864 | tf_op jit(solution)/shard_map/ppermute | solution.py:16
  292.7 55.8 %collective-permute-start.2 = (f32[6,25,32,128]{3,2,1,0:T(8,128)}, f32[6,25,32,128]{3,2,1,0:T(8,128)S(1)}, u32[]{:S(2)}, u32[]{:S(2)}) collective-permute-start(f32[6,25,32,128]{3,2,1,0:T(8,128)} %get-tuple-element.139), channel_id=1, source_target_pairs={{0,4},{4,8},{8,12},{12,16},{16,20},{20,24},{24,28},{28,0},{1,5},{5... | collective-permute-start | bytes 7372808 | tf_op jit(solution)/shard_map/ppermute | solution.py:14
  292.7 55.8 %collective-permute-start.3 = (f32[6,25,32,128]{3,2,1,0:T(8,128)}, f32[6,25,32,128]{3,2,1,0:T(8,128)}, u32[]{:S(2)}, u32[]{:S(2)}) collective-permute-start(f32[6,25,32,128]{3,2,1,0:T(8,128)} %get-tuple-element.140), channel_id=1, source_target_pairs={{4,0},{8,4},{12,8},{16,12},{20,16},{24,20},{28,24},{0,28},{5,1},{9... | collective-permute-start | bytes 7372808 | tf_op jit(solution)/shard_map/ppermute | solution.py:16
Sparse Core Ops, SparseCore 0:
  10.8 105.5 all-gather.1
where the time goes:
time: 525 us; the launch traced here: 520 us
  waiting for transfers between devices  145 us (28%)
  local copies, waits for them, and re-layouts  136 us (26%)
  matrix products  132 us (25%)
  loops' own time  46.8 us (9%)
  other arithmetic  38.1 us (7%)
  between operations  13.4 us (3%)
  starting transfers between devices  8.04 us (2%)
    ppermute x2, waiting for transfers between devices, with_halo(): lax.ppermute(tail, axis, [(i, (i + 1) % count) for i in range(count)])  78.5 us
    all_gather x1, waiting for transfers between devices, shards(): panel_piece = lax.all_gather(masked, 'col', axis=2, tiled=True)  66.3 us
    gather x12, local copies, waits for them, and re-layouts, cube_one_row(): right_blocks = square_ext[(row_index + offsets)[:, None], columns]  62 us
    dot_general x12, matrix products, cube_one_row(): jnp.einsum('sca,sibc->iba', left_blocks, right_blocks, precision=lax.Prec...  50.7 us
    dot_general x12, matrix products, square_one_row(): jnp.einsum('sca,sdbc->sdba', left_blocks, right_blocks, precision=lax.Pre...  46.2 us
    gather x12, local copies, waits for them, and re-layouts, square_one_row(): right_blocks = extended[row_index + offsets]  38.1 us
    dot_general x12, matrix products, square_one_row(): jnp.einsum('sdba,sde->eba', products, slot_place, precision=lax.Precision...  35.6 us
    another operation x1, loops' own time, shards(): square = lax.map(square_one_row, row_range)  24 us
  transfers between devices with their start and end apart: 5, of which 4 were waited for; matrix products, arithmetic and copies ran while one was open for 1% of the time, Pallas kernels for 0%

commit v1 on v0

v1 whole, which is shorter than its diff:
```python
import functools

import jax
import jax.numpy as jnp
from jax import lax
from jax.experimental import pallas as pl
from jax.experimental.pallas import tpu as pltpu
from jax.sharding import PartitionSpec as P

NZ = 7
MESH = pl.DeviceIdType.MESH


def split(x):
    hi = x.astype(jnp.bfloat16)
    return hi, (x - hi.astype(jnp.float32)).astype(jnp.bfloat16)


def dot3(lhi, llo, rhi, rlo):
    f = functools.partial(jnp.dot, preferred_element_type=jnp.float32)
    return f(lhi, rhi) + f(lhi, rlo) + f(llo, rhi)


def kernel(n_row, n_col, d_ref, pat, rank, slots, out, *scratch):
    panels = scratch[:6]
    (mext, lhi, llo, rhi, rlo, sx, shi, slo, acc, m_send, m_recv, s_send, s_recv,
     p_send, p_recv, f_send, f_recv) = scratch[6:]
    w = d_ref.shape[2]
    band = d_ref.shape[1]
    half = (band - 1) // 2
    steps = half + 1
    nb = d_ref.shape[3]
    wide = 2 * nb
    tall = (band + 1) * w
    row = lax.axis_index("row")
    col = lax.axis_index("col")
    odd = lax.rem(row, 2)
    left = lax.rem(row + n_row - 1, n_row)
    right = lax.rem(row + 1, n_row)
    outer = left + odd * (right - left)
    mate = row + 1 - 2 * odd
    grid2 = n_col == 4
    if grid2:
        xn = col + 1 - 2 * lax.rem(col, 2)
        yn = lax.rem(col + 2, 4)
        peers = [xn, yn]
    else:
        peers = [lax.rem(col + d, n_col) for d in range(1, n_col)]

    def pair(q):
        if q < 3:
            return (2 - q) + odd * (1 + 2 * q)
        return q + odd * (5 - 2 * q)

    def faces_right(q):
        return odd if q < 3 else 1 - odd

    def nbr(q):
        return outer if q < 3 else mate

    def landed(q):
        p = 5 - pair(q)
        return lax.rem(p + 9, 12)

    barrier = pltpu.get_barrier_semaphore()
    for peer in peers:
        pl.semaphore_signal(barrier, inc=1, device_id=(row, peer), device_id_type=MESH)
    for peer in (left, right):
        pl.semaphore_signal(barrier, inc=1, device_id=(peer, col), device_id_type=MESH)

    for q in range(6):
        p = pair(q)
        for dr in range(2):
            r = 2 * p + dr
            for s in range(band):
                mext[3 + p, dr, s] = d_ref[r, s] * pat[r, s].astype(jnp.float32)
            for t in range(NZ):
                panels[q][col, dr, t] = d_ref[r, slots[r, t]]

    pl.semaphore_wait(barrier, len(peers) + 2)

    def m_copy(q):
        p = pair(q)
        return pltpu.make_async_remote_copy(
            mext.at[3 + p], mext.at[lax.rem(p + 9, 12)], m_send.at[q], m_recv.at[q],
            device_id=(nbr(q), col), device_id_type=MESH)

    def m_arrival(q):
        e = landed(q)
        return pltpu.make_async_remote_copy(
            mext.at[e], mext.at[e], m_send.at[q], m_recv.at[q],
            device_id=(nbr(q), col), device_id_type=MESH)

    def s_rows(q, to_right):
        size = band + 1 + 2 * (q % 3)
        return pl.ds(pl.multiple_of(to_right * ((2 * band - size) * w), 8), size * w)

    def s_copy(q):
        p = pair(q)
        rows = s_rows(q, faces_right(q))
        return pltpu.make_async_remote_copy(
            sx.at[3 + p, rows], sx.at[lax.rem(p + 9, 12), rows], s_send.at[q], s_recv.at[q],
            device_id=(nbr(q), col), device_id_type=MESH)

    def s_arrival(q):
        e = landed(q)
        rows = s_rows(q, 1 - faces_right(q))
        return pltpu.make_async_remote_copy(
            sx.at[e, rows], sx.at[e, rows], s_send.at[q], s_recv.at[q],
            device_id=(nbr(q), col), device_id_type=MESH)

    def p_copy(q, i, who):
        return pltpu.make_async_remote_copy(
            panels[q].at[who], panels[q].at[who], p_send.at[i, q], p_recv.at[i, q],
            device_id=(row, peers[i]), device_id_type=MESH)

    def f_copy(q, i, who):
        return pltpu.make_async_remote_copy(
            panels[q].at[who, i], panels[q].at[who, i], f_send.at[i, q], f_recv.at[i, q],
            device_id=(row, peers[1 - i]), device_id_type=MESH)

    def p_start(q):
        for i in range(len(peers)):
            p_copy(q, i, col).start()

    def p_wait(q):
        for i in range(len(peers)):
            who = peers[i] if grid2 else lax.rem(col + n_col - 1 - i, n_col)
            p_copy(q, i, who).wait_recv()
        if grid2:
            for i in range(2):
                f_copy(q, i, peers[i]).start()

    for q in (0, 1):
        m_copy(2 - q).start()
        p_start(q)
    for q in (0, 5, 4, 3):
        m_copy(q).start()

    def build_left(e):
        x = mext[e]
        gap = jnp.zeros((w, nb), jnp.float32)
        first = jnp.concatenate([x[0].reshape(band * w, nb), gap], axis=0)
        second = jnp.concatenate([gap, x[1].reshape(band * w, nb)], axis=0)
        for i, part in enumerate((first, second)):
            hi, lo = split(part)
            lhi[e, :, i * nb:(i + 1) * nb] = hi
            llo[e, :, i * nb:(i + 1) * nb] = lo

    @pl.loop(0, 6)
    def _(i):
        build_left(3 + i)

    def build_right(q):
        p = pair(q)

        @pl.loop(0, steps)
        def _(m):
            for dj in range(2):
                for dr in range(2):
                    r = 2 * p + dr
                    s = 2 * m + dj - dr
                    t = rank[r, s + 1]
                    on = pat_wide(r, s)
                    x = panels[q][:, dr, t].reshape(nb, nb) * on
                    hi, lo = split(x)
                    at = (p * steps + m, pl.ds(dj * nb, nb), pl.ds(dr * nb, nb))
                    rhi[at] = hi
                    rlo[at] = lo

    def pat_wide(r, s):
        return rank[r, s + 1 + band + 2].astype(jnp.float32)

    def split_square(e, rows):
        hi, lo = split(sx[e, rows])
        shi[e, rows] = hi
        slo[e, rows] = lo

    def compute(q):
        p = pair(q)
        if grid2:
            for i in range(2):
                f_copy(q, i, 3 - col).wait_recv()
        near = 2 - q if q < 3 else 8 - q
        m_arrival(near).wait_recv()
        build_left(landed(near))
        build_right(q)
        sx[3 + p] = jnp.zeros((2 * band * w, wide), jnp.float32)

        @pl.loop(0, steps)
        def _(m):
            rows = pl.ds(pl.multiple_of(2 * m * w, 8), tall)
            k = p * steps + m
            sx[3 + p, rows] += dot3(lhi[p + m], llo[p + m], rhi[k], rlo[k])

        s_copy(q).start()
        split_square(3 + p, slice(None))

    for q in range(6):
        p_wait(q)
        if q + 2 < 6:
            p_start(q + 2)
        if q >= 1:
            compute(q - 1)
    compute(5)

    def cube(q):
        p = pair(q)
        acc[...] = jnp.zeros_like(acc)

        @pl.loop(0, steps)
        def _(m):
            rows = pl.ds(pl.multiple_of((2 * half - 2 * m) * w, 16), tall)
            e = p + m
            k = p * steps + m
            acc[...] += dot3(shi[e, rows], slo[e, rows], rhi[k], rlo[k])

        for dr in range(2):
            r = 2 * p + dr
            for i in range(band):
                lanes = pl.ds(dr * nb, nb)
                core = sx[3 + p, pl.ds((half + dr + i) * w, w), lanes]
                third = acc[pl.ds((dr + i) * w, w), lanes]
                out[r, i] = (3.0 * core - 2.0 * third) * pat[r, i].astype(jnp.float32)

    for group in ((3, 4, 5), (0, 1, 2)):
        for q in group:
            s_arrival(q).wait_recv()
            split_square(landed(q), s_rows(q, 1 - faces_right(q)))
        for q in group:
            cube(q)

    for q in range(6):
        m_copy(q).wait_send()
        s_copy(q).wait_send()
        for i in range(len(peers)):
            p_copy(q, i, col).wait_send()
        if grid2:
            for i in range(2):
                f_copy(q, i, peers[i]).wait_send()


def shards(n_row, n_col, density, pattern):
    rows, band, w, nb = density.shape
    half = (band - 1) // 2
    steps = half + 1
    slot = jnp.arange(band, dtype=jnp.int32)
    upto = jnp.sum(jnp.where(slot[None, None, :] <= slot[None, :, None], pattern[:, None, :], 0), axis=2)
    slots = jnp.sum((upto[:, None, :] <= jnp.arange(NZ, dtype=jnp.int32)[None, :, None]).astype(jnp.int32), axis=2)
    slots = jnp.clip(slots, 0, band - 1)
    rank = jnp.pad(jnp.clip(upto - 1, 0, NZ - 1), ((0, 0), (1, 1)))
    rank = jnp.concatenate([rank, jnp.pad(pattern, ((0, 0), (1, 1)))], axis=1)
    peers = 2 if n_col == 4 else n_col - 1
    tall, wide = (band + 1) * w, 2 * nb
    vmem, smem = pl.BlockSpec(memory_space=pltpu.VMEM), pl.BlockSpec(memory_space=pltpu.SMEM)
    f32, bf16, dma = jnp.float32, jnp.bfloat16, pltpu.SemaphoreType.DMA
    scratch = [pltpu.VMEM((n_col, 2, NZ, w, nb), f32) for _ in range(6)] + [
        pltpu.VMEM((12, 2, band, w, nb), f32),
        pltpu.VMEM((12, tall, wide), bf16),
        pltpu.VMEM((12, tall, wide), bf16),
        pltpu.VMEM((6 * steps, wide, wide), bf16),
        pltpu.VMEM((6 * steps, wide, wide), bf16),
        pltpu.VMEM((12, 2 * band * w, wide), f32),
        pltpu.VMEM((12, 2 * band * w, wide), bf16),
        pltpu.VMEM((12, 2 * band * w, wide), bf16),
        pltpu.VMEM((tall, wide), f32),
        dma((6,)), dma((6,)), dma((6,)), dma((6,)),
        dma((peers, 6)), dma((peers, 6)), dma((2, 6)), dma((2, 6)),
    ]
    return pl.pallas_call(
        functools.partial(kernel, n_row, n_col),
        out_shape=jax.ShapeDtypeStruct(density.shape, f32),
        in_specs=[vmem, smem, smem, smem],
        out_specs=vmem,
        scratch_shapes=scratch,
        compiler_params=pltpu.CompilerParams(
            collective_id=0, has_side_effects=True, vmem_limit_bytes=60 * 2**20),
        name="purify",
    )(density, pattern, rank, slots)


def solution(mesh):
    placed = (P("row", None, "col", None), P("row", None))
    body = functools.partial(shards, mesh.shape["row"], mesh.shape["col"])
    return jax.shard_map(
        body, mesh=mesh, in_specs=placed, out_specs=P("row", None, "col", None), check_vma=False
    )
```

time: 525 us -> 85.4 us (0.16)
  waiting for transfers between devices: 145 us -> 0 us
  local copies, waits for them, and re-layouts: 136 us -> 3.42 us
  matrix products: 132 us -> 0 us
  Pallas kernels: 0 us -> 78.5 us
  loops' own time: 46.8 us -> 0 us
  other arithmetic: 38.1 us -> 3.24 us
  between operations: 13.4 us -> 0.02 us
  starting transfers between devices: 8.04 us -> 0 us
    dot_general x36 -> x0, matrix products: 132 us -> none  [the longest x12 50.7 us: cube_one_row(): jnp.einsum('sca,sibc->iba', left_blocks, right_blocks, precision=lax.Prec...]
    gather x24 -> x0, local copies, waits for them, and re-layouts: 100 us -> none  [the longest x12 62 us: cube_one_row(): right_blocks = square_ext[(row_index + offsets)[:, None], columns]]
    ppermute x4 -> x0, waiting for transfers between devices: 79 us -> none  [the longest x2 78.5 us: with_halo(): lax.ppermute(tail, axis, [(i, (i + 1) % count) for i in range(count)])]
    pallas_call x0 -> x1, Pallas kernels: none -> 78.5 us  [shards(): pl.pallas_call(functools.partial(kernel, n_row, n_col), out_shape=jax.Sha...]
    all_gather x1 -> x0, waiting for transfers between devices: 66.3 us -> none  [shards(): panel_piece = lax.all_gather(masked, 'col', axis=2, tiled=True)]
    another operation x2 -> x0, loops' own time: 46.8 us -> none  [the longest x1 24 us: shards(): square = lax.map(square_one_row, row_range)]
    concatenate x26 -> x1, other arithmetic: 21.4 us -> 1.37 us  [shards(): rank = jnp.concatenate([rank, jnp.pad(pattern, ((0, 0), (1, 1)))], axis=1)]
    dynamic_slice x24 -> x0, local copies, waits for them, and re-layouts: 14.1 us -> none  [shards(): square = lax.map(square_one_row, row_range)]
  transfers between devices with their start and end apart: 5 -> 0, of which waited for: 4 -> 0; matrix products, arithmetic and copies ran while one was open for 1% -> 0% of each run, Pallas kernels for 0% -> 0%
where the time goes in v1:
time: 85.4 us; the launch traced here: 85.2 us
  Pallas kernels  78.5 us (92%)
  local copies, waits for them, and re-layouts  3.42 us (4%)
  other arithmetic  3.24 us (4%)
    pallas_call x1, Pallas kernels, shards(): pl.pallas_call(functools.partial(kernel, n_row, n_col), out_shape=jax.Sha...  78.5 us
    unnamed x1, local copies, waits for them, and re-layouts  3.42 us

profile of v1, /device:TPU:0, one launch (start us, length us, event | category | flops | bytes accessed | tf_op | source)
XLA Modules:
  0.0 85.2 jit_solution(11198753964318362180)
XLA Ops:
  0.0 1.0 %select_reduce_fusion = s32[12,13]{1,0:T(8,128)S(1)} fusion(s32[12,13]{1,0:T(8,128)} %pat.1, pred[13,13]{1,0:T(8,128)(4,1)S(1)} %iota_compare_fusion.1), kind=kLoop, calls=%fused_computation | loop fusion | flops 3900 | bytes 1417 | tf_op jit(solution)/shard_map/reduce_sum | solution.py:248
  1.0 0.3 convert_reduce_fusion
  1.3 1.4 %pad_add_fusion.rank = s32[12,30]{1,0:T(8,128)} fusion(s32[12,13]{1,0:T(8,128)} %pat.1, s32[12,13]{1,0:T(8,128)S(1)} %add_clamp_fusion), kind=kLoop, calls=%fused_computation.3 | loop fusion | flops 360 | bytes 2688 | tf_op jit(solution)/shard_map/concatenate | solution.py:252
  2.7 0.6 broadcast_clamp_fusion.slots
  3.3 78.5 %purify.1 = f32[12,13,32,128]{3,2,1,0:T(8,128)} custom-call(f32[12,13,32,128]{3,2,1,0:T(8,128)} %d_ref.1, s32[12,13]{1,0:T(8,128)} %pat.1, s32[12,30]{1,0:T(8,128)} %pad_add_fusion.rank, s32[12,7]{1,0:T(8,128)} %broadcast_clamp_fusion.slots), custom_call_target="tpu_custom_call" | custom-call | tf_op jit(solution)/shard_map/purify/pallas_call | solution.py:270
  81.7 3.4 %copy.4 = f32[12,13,32,128]{3,2,1,0:T(8,128)} copy(f32[12,13,32,128]{3,2,1,0:T(8,128)} %purify.1) | data formatting | bytes 5111808
  (2 shorter events, 0.0 us)

commit v2 on v1

--- a/solution.py
+++ b/solution.py
@@ -21,10 +21,10 @@
     return f(lhi, rhi) + f(lhi, rlo) + f(llo, rhi)
 
 
-def kernel(n_row, n_col, d_ref, pat, rank, slots, out, *scratch):
+def kernel(n_row, n_col, d_ref, pat, out, *scratch):
     panels = scratch[:6]
-    (mext, lhi, llo, rhi, rlo, sx, shi, slo, acc, m_send, m_recv, s_send, s_recv,
-     p_send, p_recv, f_send, f_recv) = scratch[6:]
+    (mext, lhi, llo, rhi, rlo, sx, shi, slo, acc, rank, slots, m_send, m_recv, s_send,
+     s_recv, p_send, p_recv, f_send, f_recv) = scratch[6:]
     w = d_ref.shape[2]
     band = d_ref.shape[1]
     half = (band - 1) // 2
@@ -47,10 +47,11 @@
     else:
         peers = [lax.rem(col + d, n_col) for d in range(1, n_col)]
 
+    def placed(v):
+        return v + odd * (5 - 2 * v)
+
     def pair(q):
-        if q < 3:
-            return (2 - q) + odd * (1 + 2 * q)
-        return q + odd * (5 - 2 * q)
+        return placed(2 - q if q < 3 else q)
 
     def faces_right(q):
         return odd if q < 3 else 1 - odd
@@ -68,14 +69,37 @@
     for peer in (left, right):
         pl.semaphore_signal(barrier, inc=1, device_id=(peer, col), device_id_type=MESH)
 
+    @pl.loop(0, d_ref.shape[0])
+    def _(r):
+        count = jnp.int32(0)
+        upto = []
+        for edge in (0, band + 1):
+            rank[r, edge] = jnp.int32(0)
+            rank[r, 16 + edge] = jnp.int32(0)
+        for s in range(band):
+            on = pat[r, s]
+            rank[r, s + 1] = jnp.minimum(count, NZ - 1)
+            rank[r, 16 + s + 1] = on
+            count = count + on
+            upto.append(count)
+        for t in range(NZ):
+            place = jnp.int32(0)
+            for s in range(band):
+                place = place + jnp.where(upto[s] <= t, 1, 0)
+            slots[r, t] = jnp.minimum(place, band - 1)
+
     for q in range(6):
         p = pair(q)
         for dr in range(2):
             r = 2 * p + dr
             for s in range(band):
-                mext[3 + p, dr, s] = d_ref[r, s] * pat[r, s].astype(jnp.float32)
+                mext[3 + p, dr, pl.ds(NZ * w + s, 1)] = jnp.full(
+                    (1, nb), pat[r, s].astype(jnp.float32))
+            mext[3 + p, dr, pl.ds(NZ * w + band, 16 - band)] = jnp.zeros((16 - band, nb), jnp.float32)
             for t in range(NZ):
-                panels[q][col, dr, t] = d_ref[r, slots[r, t]]
+                x = d_ref[r, slots[r, t]]
+                panels[q][col, dr, t] = x
+                mext[3 + p, dr, pl.ds(t * w, w)] = x
 
     pl.semaphore_wait(barrier, len(peers) + 2)
 
@@ -137,19 +161,42 @@
     for q in (0, 5, 4, 3):
         m_copy(q).start()
 
-    def build_left(e):
-        x = mext[e]
+    def store_left(e, blocks):
         gap = jnp.zeros((w, nb), jnp.float32)
-        first = jnp.concatenate([x[0].reshape(band * w, nb), gap], axis=0)
-        second = jnp.concatenate([gap, x[1].reshape(band * w, nb)], axis=0)
+        first = jnp.concatenate(blocks[0] + [gap], axis=0)
+        second = jnp.concatenate([gap] + blocks[1], axis=0)
         for i, part in enumerate((first, second)):
             hi, lo = split(part)
             lhi[e, :, i * nb:(i + 1) * nb] = hi
             llo[e, :, i * nb:(i + 1) * nb] = lo
 
+    def build_own(p):
+        blocks = []
+        for dr in range(2):
+            r = 2 * p + dr
+            blocks.append([d_ref[r, s] * pat[r, s].astype(jnp.float32) for s in range(band)])
+        store_left(3 + p, blocks)
+
+    def build_left(e):
+        blocks = []
+        for dr in range(2):
+            here = [jnp.ones((1, nb), jnp.float32)]
+            row_blocks = []
+            for s in range(band):
+                on = mext[e, dr, pl.ds(NZ * w + s, 1)]
+                total = jnp.zeros((w, nb), jnp.float32)
+                for t in range(max(0, s - band + NZ), min(NZ, s + 1)):
+                    total = total + (here[t] * on) * mext[e, dr, pl.ds(t * w, w)]
+                row_blocks.append(total)
+                stay = [h * (1.0 - on) for h in here] + [jnp.zeros((1, nb), jnp.float32)]
+                move = [jnp.zeros((1, nb), jnp.float32)] + [h * on for h in here]
+                here = [a + b for a, b in zip(stay, move)][:NZ]
+            blocks.append(row_blocks)
+        store_left(e, blocks)
+
     @pl.loop(0, 6)
     def _(i):
-        build_left(3 + i)
+        build_own(i)
 
     def build_right(q):
         p = pair(q)
@@ -169,7 +216,7 @@
                     rlo[at] = lo
 
     def pat_wide(r, s):
-        return rank[r, s + 1 + band + 2].astype(jnp.float32)
+        return rank[r, s + 1 + 16].astype(jnp.float32)
 
     def split_square(e, rows):
         hi, lo = split(sx[e, rows])
@@ -195,6 +242,35 @@
 
         s_copy(q).start()
         split_square(3 + p, slice(None))
+        own = 2 - q if q < 3 else q
+        low, high = (own, 2) if q < 3 else (own - 3, own)
+
+        @pl.loop(low, high + 1)
+        def _(v):
+            add_third(p, 3 + placed(v))
+
+        if high > low:
+            @pl.loop(low + 1 if q < 3 else low, high + 1 if q < 3 else high)
+            def _(v):
+                add_third(placed(v), 3 + p)
+
+    def add_third(p, e):
+        m = e - p
+        rows = pl.ds(pl.multiple_of((2 * half - 2 * m) * w, 16), tall)
+        k = p * steps + m
+        acc[p] += dot3(shi[e, rows], slo[e, rows], rhi[k], rlo[k])
+
+    def add_halo(q):
+        s_arrival(q).wait_recv()
+        e = landed(q)
+        split_square(e, s_rows(q, 1 - faces_right(q)))
+        a = q % 3
+
+        @pl.loop(0 if q < 3 else 5 - a, a + 1 if q < 3 else 6)
+        def _(v):
+            add_third(placed(v), e)
+
+    acc[...] = jnp.zeros_like(acc)
 
     for q in range(6):
         p_wait(q)
@@ -202,33 +278,27 @@
             p_start(q + 2)
         if q >= 1:
             compute(q - 1)
+    add_halo(0)
+    add_halo(1)
     compute(5)
 
-    def cube(q):
-        p = pair(q)
-        acc[...] = jnp.zeros_like(acc)
-
-        @pl.loop(0, steps)
-        def _(m):
-            rows = pl.ds(pl.multiple_of((2 * half - 2 * m) * w, 16), tall)
-            e = p + m
-            k = p * steps + m
-            acc[...] += dot3(shi[e, rows], slo[e, rows], rhi[k], rlo[k])
-
+    def finish(q):
+        p = pair(q)
         for dr in range(2):
             r = 2 * p + dr
             for i in range(band):
                 lanes = pl.ds(dr * nb, nb)
                 core = sx[3 + p, pl.ds((half + dr + i) * w, w), lanes]
-                third = acc[pl.ds((dr + i) * w, w), lanes]
+                third = acc[p, pl.ds((dr + i) * w, w), lanes]
                 out[r, i] = (3.0 * core - 2.0 * third) * pat[r, i].astype(jnp.float32)
 
-    for group in ((3, 4, 5), (0, 1, 2)):
-        for q in group:
-            s_arrival(q).wait_recv()
-            split_square(landed(q), s_rows(q, 1 - faces_right(q)))
-        for q in group:
-            cube(q)
+    add_halo(2)
+    for q in (0, 1, 2):
+        finish(q)
+    for q in (3, 4, 5):
+        add_halo(q)
+    for q in (3, 4, 5):
+        finish(q)
 
     for q in range(6):
         m_copy(q).wait_send()
@@ -242,20 +312,13 @@
 
 def shards(n_row, n_col, density, pattern):
     rows, band, w, nb = density.shape
-    half = (band - 1) // 2
-    steps = half + 1
-    slot = jnp.arange(band, dtype=jnp.int32)
-    upto = jnp.sum(jnp.where(slot[None, None, :] <= slot[None, :, None], pattern[:, None, :], 0), axis=2)
-    slots = jnp.sum((upto[:, None, :] <= jnp.arange(NZ, dtype=jnp.int32)[None, :, None]).astype(jnp.int32), axis=2)
-    slots = jnp.clip(slots, 0, band - 1)
-    rank = jnp.pad(jnp.clip(upto - 1, 0, NZ - 1), ((0, 0), (1, 1)))
-    rank = jnp.concatenate([rank, jnp.pad(pattern, ((0, 0), (1, 1)))], axis=1)
+    steps = (band + 1) // 2
     peers = 2 if n_col == 4 else n_col - 1
     tall, wide = (band + 1) * w, 2 * nb
     vmem, smem = pl.BlockSpec(memory_space=pltpu.VMEM), pl.BlockSpec(memory_space=pltpu.SMEM)
     f32, bf16, dma = jnp.float32, jnp.bfloat16, pltpu.SemaphoreType.DMA
     scratch = [pltpu.VMEM((n_col, 2, NZ, w, nb), f32) for _ in range(6)] + [
-        pltpu.VMEM((12, 2, band, w, nb), f32),
+        pltpu.VMEM((12, 2, NZ * w + 16, nb), f32),
         pltpu.VMEM((12, tall, wide), bf16),
         pltpu.VMEM((12, tall, wide), bf16),
         pltpu.VMEM((6 * steps, wide, wide), bf16),
@@ -263,20 +326,22 @@
         pltpu.VMEM((12, 2 * band * w, wide), f32),
         pltpu.VMEM((12, 2 * band * w, wide), bf16),
         pltpu.VMEM((12, 2 * band * w, wide), bf16),
-        pltpu.VMEM((tall, wide), f32),
+        pltpu.VMEM((6, tall, wide), f32),
+        pltpu.SMEM((rows, 32), jnp.int32),
+        pltpu.SMEM((rows, 8), jnp.int32),
         dma((6,)), dma((6,)), dma((6,)), dma((6,)),
         dma((peers, 6)), dma((peers, 6)), dma((2, 6)), dma((2, 6)),
     ]
     return pl.pallas_call(
         functools.partial(kernel, n_row, n_col),
         out_shape=jax.ShapeDtypeStruct(density.shape, f32),
-        in_specs=[vmem, smem, smem, smem],
+        in_specs=[vmem, smem],
         out_specs=vmem,
         scratch_shapes=scratch,
         compiler_params=pltpu.CompilerParams(
             collective_id=0, has_side_effects=True, vmem_limit_bytes=60 * 2**20),
         name="purify",
-    )(density, pattern, rank, slots)
+    )(density, pattern)
 
 
 def solution(mesh):

time: 85.4 us -> 72.5 us (0.85)
  Pallas kernels: 78.5 us -> 68.9 us
  other arithmetic: 3.24 us -> 0 us
    pallas_call x1, Pallas kernels: 78.5 us -> 68.9 us  [shards(): pl.pallas_call(functools.partial(kernel, n_row, n_col), out_shape=jax.Sha...]
    concatenate x1 -> x0, other arithmetic: 1.37 us -> none  [shards(): rank = jnp.concatenate([rank, jnp.pad(pattern, ((0, 0), (1, 1)))], axis=1)]
    reduce_sum x2 -> x0, other arithmetic: 1.26 us -> none  [the longest x1 0.97 us: shards(): jnp.sum(jnp.where(slot[None, None, :] <= slot[None, :, None], pattern[:,...]
where the time goes in v2:
time: 72.5 us; the launch traced here: 72.4 us
  Pallas kernels  68.9 us (95%)
  local copies, waits for them, and re-layouts  3.42 us (5%)
    pallas_call x1, Pallas kernels, shards(): pl.pallas_call(functools.partial(kernel, n_row, n_col), out_shape=jax.Sha...  68.9 us
    unnamed x1, local copies, waits for them, and re-layouts  3.42 us

profile of v2, /device:TPU:0, one launch (start us, length us, event | category | flops | bytes accessed | tf_op | source)
XLA Modules:
  0.0 72.4 jit_solution(13670733237985753557)
XLA Ops:
  0.0 68.9 %purify.1 = f32[12,13,32,128]{3,2,1,0:T(8,128)} custom-call(f32[12,13,32,128]{3,2,1,0:T(8,128)} %d_ref.1, s32[12,13]{1,0:T(8,128)} %pat.1), custom_call_target="tpu_custom_call" | custom-call | tf_op jit(solution)/shard_map/purify/pallas_call | solution.py:335
  68.9 3.4 %copy.4 = f32[12,13,32,128]{3,2,1,0:T(8,128)} copy(f32[12,13,32,128]{3,2,1,0:T(8,128)} %purify.1) | data formatting | bytes 5111808

commit v3 on v2

--- a/solution.py
+++ b/solution.py
@@ -17,13 +17,14 @@
 
 
 def dot3(lhi, llo, rhi, rlo):
-    f = functools.partial(jnp.dot, preferred_element_type=jnp.float32)
-    return f(lhi, rhi) + f(lhi, rlo) + f(llo, rhi)
-
-
-def kernel(n_row, n_col, d_ref, pat, out, *scratch):
+    left = jnp.concatenate([lhi, lhi, llo], axis=1)
+    right = jnp.concatenate([rhi, rlo, rhi], axis=0)
+    return jnp.dot(left, right, preferred_element_type=jnp.float32)
+
+
+def kernel(n_row, n_col, d_hbm, pat, out, *scratch):
     panels = scratch[:6]
-    (mext, lhi, llo, rhi, rlo, sx, shi, slo, acc, rank, slots, m_send, m_recv, s_send,
+    (d_ref, d_sem, mext, lhi, llo, rhi, rlo, sx, shi, slo, acc, rank, slots, m_send, m_recv, s_send,
      s_recv, p_send, p_recv, f_send, f_recv) = scratch[6:]
     w = d_ref.shape[2]
     band = d_ref.shape[1]
@@ -69,6 +70,9 @@
     for peer in (left, right):
         pl.semaphore_signal(barrier, inc=1, device_id=(peer, col), device_id_type=MESH)
 
+    fetch = pltpu.make_async_copy(d_hbm, d_ref, d_sem)
+    fetch.start()
+
     @pl.loop(0, d_ref.shape[0])
     def _(r):
         count = jnp.int32(0)
@@ -88,7 +92,62 @@
                 place = place + jnp.where(upto[s] <= t, 1, 0)
             slots[r, t] = jnp.minimum(place, band - 1)
 
-    for q in range(6):
+    fetch.wait()
+    pl.semaphore_wait(barrier, len(peers) + 2)
+
+    def m_copy(q):
+        p = pair(q)
+        return pltpu.make_async_remote_copy(
+            mext.at[3 + p], mext.at[lax.rem(p + 9, 12)], m_send.at[q], m_recv.at[q],
+            device_id=(nbr(q), col), device_id_type=MESH)
+
+    def m_arrival(q):
+        e = landed(q)
+        return pltpu.make_async_remote_copy(
+            mext.at[e], mext.at[e], m_send.at[q], m_recv.at[q],
+            device_id=(nbr(q), col), device_id_type=MESH)
+
+    def s_rows(q, to_right):
+        size = band + 1 + 2 * (q % 3)
+        return pl.ds(pl.multiple_of(to_right * ((2 * band - size) * w), 8), size * w)
+
+    def s_copy(q):
+        p = pair(q)
+        rows = s_rows(q, faces_right(q))
+        return pltpu.make_async_remote_copy(
+            sx.at[3 + p, rows], sx.at[lax.rem(p + 9, 12), rows], s_send.at[q], s_recv.at[q],
+            device_id=(nbr(q), col), device_id_type=MESH)
+
+    def s_arrival(q):
+        e = landed(q)
+        rows = s_rows(q, 1 - faces_right(q))
+        return pltpu.make_async_remote_copy(
+            sx.at[e, rows], sx.at[e, rows], s_send.at[q], s_recv.at[q],
+            device_id=(nbr(q), col), device_id_type=MESH)
+
+    def p_copy(q, i, who):
+        return pltpu.make_async_remote_copy(
+            panels[q].at[who], panels[q].at[who], p_send.at[i, q], p_recv.at[i, q],
+            device_id=(row, peers[i]), device_id_type=MESH)
+
+    def f_copy(q, i, who):
+        return pltpu.make_async_remote_copy(
+            panels[q].at[who, i], panels[q].at[who, i], f_send.at[i, q], f_recv.at[i, q],
+            device_id=(row, peers[1 - i]), device_id_type=MESH)
+
+    def p_start(q):
+        for i in range(len(peers)):
+            p_copy(q, i, col).start()
+
+    def p_wait(q):
+        for i in range(len(peers)):
+            who = peers[i] if grid2 else lax.rem(col + n_col - 1 - i, n_col)
+            p_copy(q, i, who).wait_recv()
+        if grid2:
+            for i in range(2):
+                f_copy(q, i, peers[i]).start()
+
+    def pack(q):
         p = pair(q)
         for dr in range(2):
             r = 2 * p + dr
@@ -101,64 +160,14 @@
                 panels[q][col, dr, t] = x
                 mext[3 + p, dr, pl.ds(t * w, w)] = x
 
-    pl.semaphore_wait(barrier, len(peers) + 2)
-
-    def m_copy(q):
-        p = pair(q)
-        return pltpu.make_async_remote_copy(
-            mext.at[3 + p], mext.at[lax.rem(p + 9, 12)], m_send.at[q], m_recv.at[q],
-            device_id=(nbr(q), col), device_id_type=MESH)
-
-    def m_arrival(q):
-        e = landed(q)
-        return pltpu.make_async_remote_copy(
-            mext.at[e], mext.at[e], m_send.at[q], m_recv.at[q],
-            device_id=(nbr(q), col), device_id_type=MESH)
-
-    def s_rows(q, to_right):
-        size = band + 1 + 2 * (q % 3)
-        return pl.ds(pl.multiple_of(to_right * ((2 * band - size) * w), 8), size * w)
-
-    def s_copy(q):
-        p = pair(q)
-        rows = s_rows(q, faces_right(q))
-        return pltpu.make_async_remote_copy(
-            sx.at[3 + p, rows], sx.at[lax.rem(p + 9, 12), rows], s_send.at[q], s_recv.at[q],
-            device_id=(nbr(q), col), device_id_type=MESH)
-
-    def s_arrival(q):
-        e = landed(q)
-        rows = s_rows(q, 1 - faces_right(q))
-        return pltpu.make_async_remote_copy(
-            sx.at[e, rows], sx.at[e, rows], s_send.at[q], s_recv.at[q],
-            device_id=(nbr(q), col), device_id_type=MESH)
-
-    def p_copy(q, i, who):
-        return pltpu.make_async_remote_copy(
-            panels[q].at[who], panels[q].at[who], p_send.at[i, q], p_recv.at[i, q],
-            device_id=(row, peers[i]), device_id_type=MESH)
-
-    def f_copy(q, i, who):
-        return pltpu.make_async_remote_copy(
-            panels[q].at[who, i], panels[q].at[who, i], f_send.at[i, q], f_recv.at[i, q],
-            device_id=(row, peers[1 - i]), device_id_type=MESH)
-
-    def p_start(q):
-        for i in range(len(peers)):
-            p_copy(q, i, col).start()
-
-    def p_wait(q):
-        for i in range(len(peers)):
-            who = peers[i] if grid2 else lax.rem(col + n_col - 1 - i, n_col)
-            p_copy(q, i, who).wait_recv()
-        if grid2:
-            for i in range(2):
-                f_copy(q, i, peers[i]).start()
-
     for q in (0, 1):
-        m_copy(2 - q).start()
+        pack(q)
         p_start(q)
-    for q in (0, 5, 4, 3):
+    pack(2)
+    for q in (2, 1, 0):
+        m_copy(q).start()
+    for q in (5, 4, 3):
+        pack(q)
         m_copy(q).start()
 
     def store_left(e, blocks):
@@ -318,6 +327,8 @@
     vmem, smem = pl.BlockSpec(memory_space=pltpu.VMEM), pl.BlockSpec(memory_space=pltpu.SMEM)
     f32, bf16, dma = jnp.float32, jnp.bfloat16, pltpu.SemaphoreType.DMA
     scratch = [pltpu.VMEM((n_col, 2, NZ, w, nb), f32) for _ in range(6)] + [
+        pltpu.VMEM(density.shape, f32),
+        dma,
         pltpu.VMEM((12, 2, NZ * w + 16, nb), f32),
         pltpu.VMEM((12, tall, wide), bf16),
         pltpu.VMEM((12, tall, wide), bf16),
@@ -334,8 +345,8 @@
     ]
     return pl.pallas_call(
         functools.partial(kernel, n_row, n_col),
-        out_shape=jax.ShapeDtypeStruct(density.shape, f32),
-        in_specs=[vmem, smem],
+        out_shape=pltpu.VMEM(density.shape, f32),
+        in_specs=[pl.BlockSpec(memory_space=pl.ANY), smem],
         out_specs=vmem,
         scratch_shapes=scratch,
         compiler_params=pltpu.CompilerParams(

time: 72.5 us -> 68.3 us (0.942)
  Pallas kernels: 68.9 us -> 66.6 us
  local copies, waits for them, and re-layouts: 3.42 us -> 1.47 us
    pallas_call x1, Pallas kernels: 68.9 us -> 66.6 us  [shards(): pl.pallas_call(functools.partial(kernel, n_row, n_col), out_shape=pltpu.V...]
    unnamed x1, local copies, waits for them, and re-layouts: 3.42 us -> 1.47 us
where the time goes in v3:
time: 68.3 us; the launch traced here: 68.1 us
  Pallas kernels  66.6 us (98%)
  local copies, waits for them, and re-layouts  1.47 us (2%)
    pallas_call x1, Pallas kernels, shards(): pl.pallas_call(functools.partial(kernel, n_row, n_col), out_shape=pltpu.V...  66.6 us
    unnamed x1, local copies, waits for them, and re-layouts  1.47 us

profile of v3, /device:TPU:0, one launch (start us, length us, event | category | flops | bytes accessed | tf_op | source)
XLA Modules:
  0.0 68.1 jit_solution(16538431847132040166)
XLA Ops:
  0.0 66.6 %purify.1 = f32[12,13,32,128]{3,2,1,0:T(8,128)S(1)} custom-call(f32[12,13,32,128]{3,2,1,0:T(8,128)} %d_hbm.1, s32[12,13]{1,0:T(8,128)} %pat.1), custom_call_target="tpu_custom_call" | custom-call | tf_op jit(solution)/shard_map/purify/pallas_call | solution.py:346
  66.6 1.5 %copy.4 = f32[12,13,32,128]{3,2,1,0:T(8,128)} copy(f32[12,13,32,128]{3,2,1,0:T(8,128)S(1)} %purify.1) | data formatting | bytes 5111808

commit v4 on v3

--- a/solution.py
+++ b/solution.py
@@ -125,9 +125,10 @@
             sx.at[e, rows], sx.at[e, rows], s_send.at[q], s_recv.at[q],
             device_id=(nbr(q), col), device_id_type=MESH)
 
-    def p_copy(q, i, who):
-        return pltpu.make_async_remote_copy(
-            panels[q].at[who], panels[q].at[who], p_send.at[i, q], p_recv.at[i, q],
+    def p_copy(q, i, who, part):
+        at = panels[q].at[who, (i + part) % 2]
+        return pltpu.make_async_remote_copy(
+            at, at, p_send.at[i, part, q], p_recv.at[i, part, q],
             device_id=(row, peers[i]), device_id_type=MESH)
 
     def f_copy(q, i, who):
@@ -136,16 +137,16 @@
             device_id=(row, peers[1 - i]), device_id_type=MESH)
 
     def p_start(q):
-        for i in range(len(peers)):
-            p_copy(q, i, col).start()
-
-    def p_wait(q):
+        for part in range(2):
+            for i in range(len(peers)):
+                p_copy(q, i, col, part).start()
+
+    def p_wait(q, part):
         for i in range(len(peers)):
             who = peers[i] if grid2 else lax.rem(col + n_col - 1 - i, n_col)
-            p_copy(q, i, who).wait_recv()
-        if grid2:
-            for i in range(2):
-                f_copy(q, i, peers[i]).start()
+            p_copy(q, i, who, part).wait_recv()
+            if grid2 and part == 0:
+                f_copy(q, i, who).start()
 
     def pack(q):
         p = pair(q)
@@ -234,6 +235,7 @@
 
     def compute(q):
         p = pair(q)
+        p_wait(q, 1)
         if grid2:
             for i in range(2):
                 f_copy(q, i, 3 - col).wait_recv()
@@ -282,7 +284,7 @@
     acc[...] = jnp.zeros_like(acc)
 
     for q in range(6):
-        p_wait(q)
+        p_wait(q, 0)
         if q + 2 < 6:
             p_start(q + 2)
         if q >= 1:
@@ -313,7 +315,8 @@
         m_copy(q).wait_send()
         s_copy(q).wait_send()
         for i in range(len(peers)):
-            p_copy(q, i, col).wait_send()
+            for part in range(2):
+                p_copy(q, i, col, part).wait_send()
         if grid2:
             for i in range(2):
                 f_copy(q, i, peers[i]).wait_send()
@@ -341,7 +344,7 @@
         pltpu.SMEM((rows, 32), jnp.int32),
         pltpu.SMEM((rows, 8), jnp.int32),
         dma((6,)), dma((6,)), dma((6,)), dma((6,)),
-        dma((peers, 6)), dma((peers, 6)), dma((2, 6)), dma((2, 6)),
+        dma((peers, 2, 6)), dma((peers, 2, 6)), dma((2, 6)), dma((2, 6)),
     ]
     return pl.pallas_call(
         functools.partial(kernel, n_row, n_col),

time: 68.3 us -> 68.5 us (level)
  no operation moved by 1% of the time
where the time goes in v4:
time: 68.5 us; the launch traced here: 68.3 us
  Pallas kernels  66.8 us (98%)
  local copies, waits for them, and re-layouts  1.47 us (2%)
    pallas_call x1, Pallas kernels, shards(): pl.pallas_call(functools.partial(kernel, n_row, n_col), out_shape=pltpu.V...  66.8 us
    unnamed x1, local copies, waits for them, and re-layouts  1.47 us

profile of v4, /device:TPU:0, one launch (start us, length us, event | category | flops | bytes accessed | tf_op | source)
XLA Modules:
  0.0 68.3 jit_solution(9955672027612240983)
XLA Ops:
  0.0 66.8 %purify.1 = f32[12,13,32,128]{3,2,1,0:T(8,128)S(1)} custom-call(f32[12,13,32,128]{3,2,1,0:T(8,128)} %d_hbm.1, s32[12,13]{1,0:T(8,128)} %pat.1), custom_call_target="tpu_custom_call" | custom-call | tf_op jit(solution)/shard_map/purify/pallas_call | solution.py:349
  66.8 1.5 %copy.4 = f32[12,13,32,128]{3,2,1,0:T(8,128)} copy(f32[12,13,32,128]{3,2,1,0:T(8,128)S(1)} %purify.1) | data formatting | bytes 5111808

commit v5 on v4

--- a/solution.py
+++ b/solution.py
@@ -54,6 +54,17 @@
     def pair(q):
         return placed(2 - q if q < 3 else q)
 
+    def own_place(q):
+        late = lax.div(q, 3)
+        return (1 - late) * (2 - q) + late * q
+
+    def near_place(q):
+        late = lax.div(q, 3)
+        return (1 - late) * q + late * (8 - q)
+
+    def landed_at(v):
+        return lax.rem(14 - placed(v), 12)
+
     def faces_right(q):
         return odd if q < 3 else 1 - odd
 
@@ -233,83 +244,82 @@
         shi[e, rows] = hi
         slo[e, rows] = lo
 
-    def compute(q):
-        p = pair(q)
+    def arrive(q):
+        if q + 1 < 6:
+            p_wait(q + 1, 0)
+        if q + 3 < 6:
+            p_start(q + 3)
         p_wait(q, 1)
         if grid2:
             for i in range(2):
                 f_copy(q, i, 3 - col).wait_recv()
-        near = 2 - q if q < 3 else 8 - q
-        m_arrival(near).wait_recv()
-        build_left(landed(near))
+        m_arrival(2 - q if q < 3 else 8 - q).wait_recv()
         build_right(q)
-        sx[3 + p] = jnp.zeros((2 * band * w, wide), jnp.float32)
-
-        @pl.loop(0, steps)
-        def _(m):
-            rows = pl.ds(pl.multiple_of(2 * m * w, 8), tall)
-            k = p * steps + m
-            sx[3 + p, rows] += dot3(lhi[p + m], llo[p + m], rhi[k], rlo[k])
-
-        s_copy(q).start()
-        split_square(3 + p, slice(None))
-        own = 2 - q if q < 3 else q
-        low, high = (own, 2) if q < 3 else (own - 3, own)
-
-        @pl.loop(low, high + 1)
-        def _(v):
-            add_third(p, 3 + placed(v))
-
-        if high > low:
-            @pl.loop(low + 1 if q < 3 else low, high + 1 if q < 3 else high)
-            def _(v):
-                add_third(placed(v), 3 + p)
-
-    def add_third(p, e):
+
+    def case(index, branch):
+        for q in range(6):
+            pl.when(index == q)(functools.partial(branch, q))
+
+    def third(p, e):
         m = e - p
         rows = pl.ds(pl.multiple_of((2 * half - 2 * m) * w, 16), tall)
         k = p * steps + m
-        acc[p] += dot3(shi[e, rows], slo[e, rows], rhi[k], rlo[k])
-
-    def add_halo(q):
+        return dot3(shi[e, rows], slo[e, rows], rhi[k], rlo[k])
+
+    def step(q):
+        case(q, arrive)
+        v0 = own_place(q)
+        p = placed(v0)
+        build_left(landed_at(near_place(q)))
+        sx[3 + p] = jnp.zeros((2 * band * w, wide), jnp.float32)
+        for m in range(steps):
+            k = p * steps + m
+            sx[3 + p, pl.ds(2 * m * w, tall)] += dot3(lhi[p + m], llo[p + m], rhi[k], rlo[k])
+        case(q, lambda i: s_copy(i).start())
+        split_square(3 + p, slice(None))
+        acc[p] += third(p, 3 + p)
+        late = lax.div(q, 3)
+        low = (1 - late) * (v0 + 1) + late * (q - 3)
+        high = (1 - late) * 3 + late * q
+
+        @pl.loop(low, high)
+        def _(v):
+            pv = placed(v)
+            a, b = third(p, 3 + pv), third(pv, 3 + p)
+            acc[p] += a
+            acc[pv] += b
+
+    def halo_in(q):
         s_arrival(q).wait_recv()
-        e = landed(q)
-        split_square(e, s_rows(q, 1 - faces_right(q)))
-        a = q % 3
-
-        @pl.loop(0 if q < 3 else 5 - a, a + 1 if q < 3 else 6)
+        split_square(landed(q), s_rows(q, 1 - faces_right(q)))
+
+    def halo_step(q):
+        case(q, halo_in)
+        late = lax.div(q, 3)
+        e = landed_at(own_place(q))
+        a = q - 3 * late
+
+        @pl.loop(late * (5 - a), late * 6 + (1 - late) * (a + 1))
         def _(v):
-            add_third(placed(v), e)
+            p = placed(v)
+            acc[p] += third(p, e)
 
     acc[...] = jnp.zeros_like(acc)
 
-    for q in range(6):
-        p_wait(q, 0)
-        if q + 2 < 6:
-            p_start(q + 2)
-        if q >= 1:
-            compute(q - 1)
-    add_halo(0)
-    add_halo(1)
-    compute(5)
-
-    def finish(q):
-        p = pair(q)
+    p_wait(0, 0)
+    p_start(2)
+    pl.loop(0, 6)(step)
+    pl.loop(0, 6)(halo_step)
+
+    @pl.loop(0, 6)
+    def _(p):
         for dr in range(2):
             r = 2 * p + dr
             for i in range(band):
                 lanes = pl.ds(dr * nb, nb)
                 core = sx[3 + p, pl.ds((half + dr + i) * w, w), lanes]
-                third = acc[p, pl.ds((dr + i) * w, w), lanes]
-                out[r, i] = (3.0 * core - 2.0 * third) * pat[r, i].astype(jnp.float32)
-
-    add_halo(2)
-    for q in (0, 1, 2):
-        finish(q)
-    for q in (3, 4, 5):
-        add_halo(q)
-    for q in (3, 4, 5):
-        finish(q)
+                cube = acc[p, pl.ds((dr + i) * w, w), lanes]
+                out[r, i] = (3.0 * core - 2.0 * cube) * pat[r, i].astype(jnp.float32)
 
     for q in range(6):
         m_copy(q).wait_send()

time: 68.5 us -> 66.5 us (0.971)
  Pallas kernels: 66.8 us -> 64.9 us
    pallas_call x1, Pallas kernels: 66.8 us -> 64.9 us  [shards(): pl.pallas_call(functools.partial(kernel, n_row, n_col), out_shape=pltpu.V...]
where the time goes in v5:
time: 66.5 us; the launch traced here: 66.3 us
  Pallas kernels  64.9 us (98%)
  local copies, waits for them, and re-layouts  1.47 us (2%)
    pallas_call x1, Pallas kernels, shards(): pl.pallas_call(functools.partial(kernel, n_row, n_col), out_shape=pltpu.V...  64.9 us
    unnamed x1, local copies, waits for them, and re-layouts  1.47 us

profile of v5, /device:TPU:0, one launch (start us, length us, event | category | flops | bytes accessed | tf_op | source)
XLA Modules:
  0.0 66.3 jit_solution(13551046671043668658)
XLA Ops:
  0.0 64.9 %purify.1 = f32[12,13,32,128]{3,2,1,0:T(8,128)S(1)} custom-call(f32[12,13,32,128]{3,2,1,0:T(8,128)} %d_hbm.1, s32[12,13]{1,0:T(8,128)} %pat.1), custom_call_target="tpu_custom_call" | custom-call | tf_op jit(solution)/shard_map/purify/pallas_call | solution.py:359
  64.9 1.5 %copy.4 = f32[12,13,32,128]{3,2,1,0:T(8,128)} copy(f32[12,13,32,128]{3,2,1,0:T(8,128)S(1)} %purify.1) | data formatting | bytes 5111808

commit v6 on v5

--- a/solution.py
+++ b/solution.py
@@ -84,8 +84,63 @@
     fetch = pltpu.make_async_copy(d_hbm, d_ref, d_sem)
     fetch.start()
 
-    @pl.loop(0, d_ref.shape[0])
-    def _(r):
+    fetch.wait()
+    pl.semaphore_wait(barrier, len(peers) + 2)
+
+    def m_copy(q):
+        p = pair(q)
+        return pltpu.make_async_remote_copy(
+            mext.at[3 + p], mext.at[lax.rem(p + 9, 12)], m_send.at[q], m_recv.at[q],
+            device_id=(nbr(q), col), device_id_type=MESH)
+
+    def m_arrival(q):
+        e = landed(q)
+        return pltpu.make_async_remote_copy(
+            mext.at[e], mext.at[e], m_send.at[q], m_recv.at[q],
+            device_id=(nbr(q), col), device_id_type=MESH)
+
+    def s_rows(q, to_right):
+        size = band + 1 + 2 * (q % 3)
+        return pl.ds(pl.multiple_of(to_right * ((2 * band - size) * w), 8), size * w)
+
+    def s_copy(q):
+        p = pair(q)
+        rows = s_rows(q, faces_right(q))
+        return pltpu.make_async_remote_copy(
+            sx.at[3 + p, rows], sx.at[lax.rem(p + 9, 12), rows], s_send.at[q], s_recv.at[q],
+            device_id=(nbr(q), col), device_id_type=MESH)
+
+    def s_arrival(q):
+        e = landed(q)
+        rows = s_rows(q, 1 - faces_right(q))
+        return pltpu.make_async_remote_copy(
+            sx.at[e, rows], sx.at[e, rows], s_send.at[q], s_recv.at[q],
+            device_id=(nbr(q), col), device_id_type=MESH)
+
+    def p_copy(q, i, who, part):
+        at = panels[q].at[who, (i + part) % 2]
+        return pltpu.make_async_remote_copy(
+            at, at, p_send.at[i, part, q], p_recv.at[i, part, q],
+            device_id=(row, peers[i]), device_id_type=MESH)
+
+    def f_copy(q, i, who):
+        return pltpu.make_async_remote_copy(
+            panels[q].at[who, i], panels[q].at[who, i], f_send.at[i, q], f_recv.at[i, q],
+            device_id=(row, peers[1 - i]), device_id_type=MESH)
+
+    def p_start(q):
+        for part in range(2):
+            for i in range(len(peers)):
+                p_copy(q, i, col, part).start()
+
+    def p_wait(q, part):
+        for i in range(len(peers)):
+            who = peers[i] if grid2 else lax.rem(col + n_col - 1 - i, n_col)
+            p_copy(q, i, who, part).wait_recv()
+            if grid2 and part == 0:
+                f_copy(q, i, who).start()
+
+    def tables(r):
         count = jnp.int32(0)
         upto = []
         for edge in (0, band + 1):
@@ -103,63 +158,8 @@
                 place = place + jnp.where(upto[s] <= t, 1, 0)
             slots[r, t] = jnp.minimum(place, band - 1)
 
-    fetch.wait()
-    pl.semaphore_wait(barrier, len(peers) + 2)
-
-    def m_copy(q):
-        p = pair(q)
-        return pltpu.make_async_remote_copy(
-            mext.at[3 + p], mext.at[lax.rem(p + 9, 12)], m_send.at[q], m_recv.at[q],
-            device_id=(nbr(q), col), device_id_type=MESH)
-
-    def m_arrival(q):
-        e = landed(q)
-        return pltpu.make_async_remote_copy(
-            mext.at[e], mext.at[e], m_send.at[q], m_recv.at[q],
-            device_id=(nbr(q), col), device_id_type=MESH)
-
-    def s_rows(q, to_right):
-        size = band + 1 + 2 * (q % 3)
-        return pl.ds(pl.multiple_of(to_right * ((2 * band - size) * w), 8), size * w)
-
-    def s_copy(q):
-        p = pair(q)
-        rows = s_rows(q, faces_right(q))
-        return pltpu.make_async_remote_copy(
-            sx.at[3 + p, rows], sx.at[lax.rem(p + 9, 12), rows], s_send.at[q], s_recv.at[q],
-            device_id=(nbr(q), col), device_id_type=MESH)
-
-    def s_arrival(q):
-        e = landed(q)
-        rows = s_rows(q, 1 - faces_right(q))
-        return pltpu.make_async_remote_copy(
-            sx.at[e, rows], sx.at[e, rows], s_send.at[q], s_recv.at[q],
-            device_id=(nbr(q), col), device_id_type=MESH)
-
-    def p_copy(q, i, who, part):
-        at = panels[q].at[who, (i + part) % 2]
-        return pltpu.make_async_remote_copy(
-            at, at, p_send.at[i, part, q], p_recv.at[i, part, q],
-            device_id=(row, peers[i]), device_id_type=MESH)
-
-    def f_copy(q, i, who):
-        return pltpu.make_async_remote_copy(
-            panels[q].at[who, i], panels[q].at[who, i], f_send.at[i, q], f_recv.at[i, q],
-            device_id=(row, peers[1 - i]), device_id_type=MESH)
-
-    def p_start(q):
-        for part in range(2):
-            for i in range(len(peers)):
-                p_copy(q, i, col, part).start()
-
-    def p_wait(q, part):
-        for i in range(len(peers)):
-            who = peers[i] if grid2 else lax.rem(col + n_col - 1 - i, n_col)
-            p_copy(q, i, who, part).wait_recv()
-            if grid2 and part == 0:
-                f_copy(q, i, who).start()
-
     def pack(q):
+        pl.loop(2 * pair(q), 2 * pair(q) + 2)(tables)
         p = pair(q)
         for dr in range(2):
             r = 2 * p + dr
@@ -245,10 +245,12 @@
         slo[e, rows] = lo
 
     def arrive(q):
-        if q + 1 < 6:
+        if q + 1 < 5:
             p_wait(q + 1, 0)
-        if q + 3 < 6:
+        if q + 3 < 5:
             p_start(q + 3)
+        if q == 3:
+            p_start(5)
         p_wait(q, 1)
         if grid2:
             for i in range(2):
@@ -266,7 +268,13 @@
         k = p * steps + m
         return dot3(shi[e, rows], slo[e, rows], rhi[k], rlo[k])
 
+    def leave(q):
+        s_copy(q).start()
+        if q == 4:
+            p_wait(5, 0)
+
     def step(q):
+        pl.when(q == 4)(lambda: pl.loop(0, 3)(halo_step))
         case(q, arrive)
         v0 = own_place(q)
         p = placed(v0)
@@ -275,7 +283,7 @@
         for m in range(steps):
             k = p * steps + m
             sx[3 + p, pl.ds(2 * m * w, tall)] += dot3(lhi[p + m], llo[p + m], rhi[k], rlo[k])
-        case(q, lambda i: s_copy(i).start())
+        case(q, leave)
         split_square(3 + p, slice(None))
         acc[p] += third(p, 3 + p)
         late = lax.div(q, 3)
@@ -309,7 +317,7 @@
     p_wait(0, 0)
     p_start(2)
     pl.loop(0, 6)(step)
-    pl.loop(0, 6)(halo_step)
+    pl.loop(3, 6)(halo_step)
 
     @pl.loop(0, 6)
     def _(p):

time: 66.5 us -> 75 us (1.13)
  Pallas kernels: 64.9 us -> 73.1 us
    pallas_call x1, Pallas kernels: 64.9 us -> 73.1 us  [shards(): pl.pallas_call(functools.partial(kernel, n_row, n_col), out_shape=pltpu.V...]
where the time goes in v6:
time: 75 us; the launch traced here: 74.6 us
  Pallas kernels  73.1 us (97%)
  local copies, waits for them, and re-layouts  1.47 us (2%)
    pallas_call x1, Pallas kernels, shards(): pl.pallas_call(functools.partial(kernel, n_row, n_col), out_shape=pltpu.V...  73.1 us

profile of v6, /device:TPU:0, one launch (start us, length us, event | category | flops | bytes accessed | tf_op | source)
XLA Modules:
  0.0 74.6 jit_solution(11369575032136786523)
XLA Ops:
  0.0 73.1 %purify.1 = f32[12,13,32,128]{3,2,1,0:T(8,128)S(1)} custom-call(f32[12,13,32,128]{3,2,1,0:T(8,128)} %d_hbm.1, s32[12,13]{1,0:T(8,128)} %pat.1), custom_call_target="tpu_custom_call" | custom-call | tf_op jit(solution)/shard_map/purify/pallas_call | solution.py:367
  73.1 1.5 %copy.4 = f32[12,13,32,128]{3,2,1,0:T(8,128)} copy(f32[12,13,32,128]{3,2,1,0:T(8,128)S(1)} %purify.1) | data formatting | bytes 5111808

commit v7 on v6

--- a/solution.py
+++ b/solution.py
@@ -172,11 +172,12 @@
                 panels[q][col, dr, t] = x
                 mext[3 + p, dr, pl.ds(t * w, w)] = x
 
+    pack(2)
+    m_copy(2).start()
     for q in (0, 1):
         pack(q)
         p_start(q)
-    pack(2)
-    for q in (2, 1, 0):
+    for q in (1, 0):
         m_copy(q).start()
     for q in (5, 4, 3):
         pack(q)
@@ -244,13 +245,17 @@
         shi[e, rows] = hi
         slo[e, rows] = lo
 
-    def arrive(q):
-        if q + 1 < 5:
+    def pass_on(q):
+        if q + 1 < 6:
             p_wait(q + 1, 0)
         if q + 3 < 5:
             p_start(q + 3)
         if q == 3:
             p_start(5)
+
+    def arrive(q):
+        if q not in (0, 4):
+            pass_on(q)
         p_wait(q, 1)
         if grid2:
             for i in range(2):
@@ -270,11 +275,10 @@
 
     def leave(q):
         s_copy(q).start()
-        if q == 4:
-            p_wait(5, 0)
+        if q in (0, 4):
+            pass_on(q)
 
     def step(q):
-        pl.when(q == 4)(lambda: pl.loop(0, 3)(halo_step))
         case(q, arrive)
         v0 = own_place(q)
         p = placed(v0)
@@ -317,10 +321,10 @@
     p_wait(0, 0)
     p_start(2)
     pl.loop(0, 6)(step)
-    pl.loop(3, 6)(halo_step)
-
-    @pl.loop(0, 6)
-    def _(p):
+    pl.loop(0, 5)(lambda i: halo_step(i + lax.div(i + 1, 3)))
+
+    def finish(v):
+        p = placed(v)
         for dr in range(2):
             r = 2 * p + dr
             for i in range(band):
@@ -328,6 +332,10 @@
                 core = sx[3 + p, pl.ds((half + dr + i) * w, w), lanes]
                 cube = acc[p, pl.ds((dr + i) * w, w), lanes]
                 out[r, i] = (3.0 * core - 2.0 * cube) * pat[r, i].astype(jnp.float32)
+
+    pl.loop(3, 6)(finish)
+    pl.loop(2, 3)(halo_step)
+    pl.loop(0, 3)(finish)
 
     for q in range(6):
         m_copy(q).wait_send()

time: 75 us -> 67.1 us (0.89)
  Pallas kernels: 73.1 us -> 65.4 us
    pallas_call x1, Pallas kernels: 73.1 us -> 65.4 us  [shards(): pl.pallas_call(functools.partial(kernel, n_row, n_col), out_shape=pltpu.V...]
where the time goes in v7:
time: 67.1 us; the launch traced here: 66.9 us
  Pallas kernels  65.4 us (97%)
  local copies, waits for them, and re-layouts  1.47 us (2%)
    pallas_call x1, Pallas kernels, shards(): pl.pallas_call(functools.partial(kernel, n_row, n_col), out_shape=pltpu.V...  65.4 us
    unnamed x1, local copies, waits for them, and re-layouts  1.47 us

profile of v7, /device:TPU:0, one launch (start us, length us, event | category | flops | bytes accessed | tf_op | source)
XLA Modules:
  0.0 66.9 jit_solution(5566031888231810445)
XLA Ops:
  0.0 65.4 %purify.1 = f32[12,13,32,128]{3,2,1,0:T(8,128)S(1)} custom-call(f32[12,13,32,128]{3,2,1,0:T(8,128)} %d_hbm.1, s32[12,13]{1,0:T(8,128)} %pat.1), custom_call_target="tpu_custom_call" | custom-call | tf_op jit(solution)/shard_map/purify/pallas_call | solution.py:375
  65.4 1.5 %copy.4 = f32[12,13,32,128]{3,2,1,0:T(8,128)} copy(f32[12,13,32,128]{3,2,1,0:T(8,128)S(1)} %purify.1) | data formatting | bytes 5111808

commit v8 on v7

--- a/solution.py
+++ b/solution.py
@@ -279,6 +279,7 @@
             pass_on(q)
 
     def step(q):
+        pl.when(q == 5)(lambda: pl.loop(0, 2)(halo_step))
         case(q, arrive)
         v0 = own_place(q)
         p = placed(v0)
@@ -321,7 +322,7 @@
     p_wait(0, 0)
     p_start(2)
     pl.loop(0, 6)(step)
-    pl.loop(0, 5)(lambda i: halo_step(i + lax.div(i + 1, 3)))
+    pl.loop(3, 6)(halo_step)
 
     def finish(v):
         p = placed(v)

time: 67.1 us -> 65.8 us (0.981)
  Pallas kernels: 65.4 us -> 64.1 us
    pallas_call x1, Pallas kernels: 65.4 us -> 64.1 us  [shards(): pl.pallas_call(functools.partial(kernel, n_row, n_col), out_shape=pltpu.V...]
where the time goes in v8:
time: 65.8 us; the launch traced here: 65.6 us
  Pallas kernels  64.1 us (97%)
  local copies, waits for them, and re-layouts  1.47 us (2%)
    pallas_call x1, Pallas kernels, shards(): pl.pallas_call(functools.partial(kernel, n_row, n_col), out_shape=pltpu.V...  64.1 us
    unnamed x1, local copies, waits for them, and re-layouts  1.47 us

profile of v8, /device:TPU:0, one launch (start us, length us, event | category | flops | bytes accessed | tf_op | source)
XLA Modules:
  0.0 65.6 jit_solution(9030842070321810391)
XLA Ops:
  0.0 64.1 %purify.1 = f32[12,13,32,128]{3,2,1,0:T(8,128)S(1)} custom-call(f32[12,13,32,128]{3,2,1,0:T(8,128)} %d_hbm.1, s32[12,13]{1,0:T(8,128)} %pat.1), custom_call_target="tpu_custom_call" | custom-call | tf_op jit(solution)/shard_map/purify/pallas_call | solution.py:376
  64.1 1.5 %copy.4 = f32[12,13,32,128]{3,2,1,0:T(8,128)} copy(f32[12,13,32,128]{3,2,1,0:T(8,128)S(1)} %purify.1) | data formatting | bytes 5111808
